TPU v7x, 128 devices: a whole 4x4x4 slice. The times are simulated.
128 devices in a mesh: expert: 64 (over z, y, x_hi, core), dp: 2 (over x_lo).
Axes of the slice: x: 4 (x_hi: 2, x_lo: 2; x = x_hi * 2 + x_lo), y: 4, z: 4, core: 2. Of those that a mesh axis runs over, the one named last changes fastest.
Arguments:
- activations: bfloat16 [16384, 3584], P(('expert', 'dp')), may hold values from -6 to 6
- out_grad: bfloat16 [16384, 3584], P(('expert', 'dp')), may hold values from -1.5 to 1.5
- expert_ids: int32 [16384, 1], P(('expert', 'dp')), may hold values from 0 to 63; in each aligned block of 128 rows (0 to 127, 128 to 255, ...) at most 6 rows name the same one
- gate_probs: bfloat16 [16384, 1], P(('expert', 'dp')), may hold values from 0.049804688 to 1
- gate_weight: bfloat16 [64, 3584, 1024], P('expert', 'dp'), may hold values from -0.09375 to 0.09375
- up_weight: bfloat16 [64, 3584, 1024], P('expert', 'dp'), may hold values from -0.09375 to 0.09375
- down_weight: bfloat16 [64, 3584, 1024], P('expert', 'dp'), may hold values from -0.1875 to 0.1875
Outputs:
- input_delta: bfloat16 [16384, 3584], P(('expert', 'dp'))
- prob_delta: bfloat16 [16384, 1], P(('expert', 'dp'))
- gate_delta: bfloat16 [64, 3584, 1024], P('expert', 'dp')
- up_delta: bfloat16 [64, 3584, 1024], P('expert', 'dp')
- down_delta: bfloat16 [64, 3584, 1024], P('expert', 'dp')
Inputs may be any that keep to these rules, and one draw needn't show every extreme that they name: `expert_ids`: among the 128 tokens of one device (aligned blocks of rows), no expert is named more than 6 times, a bound that some block reaches.
All inputs are finite; a program needn't handle non-finite values.
Results may differ from a plain program's by a relative error of at most 0.034.
Values may be sent and summed in bfloat16 or wider, within the bound.
A program may use at most 128 MiB of HBM per device.

v0:
```python
import jax
import jax.numpy as jnp
from jax import lax
from jax.sharding import PartitionSpec as P


def activate(summed, prob_rows, hidden):
    pre_gate = summed[:, :hidden]
    pre_up = summed[:, hidden : 2 * hidden]
    raw_grad = summed[:, 2 * hidden :]
    sigmoid_gate = jax.nn.sigmoid(pre_gate)
    silu_gate = pre_gate * sigmoid_gate
    hidden_rows = (silu_gate * pre_up).astype(jnp.bfloat16)
    scaled_grad = prob_rows.astype(jnp.float32)[:, None] * raw_grad
    slope = sigmoid_gate * (1.0 + pre_gate * (1.0 - sigmoid_gate))
    gate_rows = (scaled_grad * pre_up * slope).astype(jnp.bfloat16)
    up_rows = (scaled_grad * silu_gate).astype(jnp.bfloat16)
    return (hidden_rows, gate_rows, up_rows)


def on_device(activations, out_grad, expert_ids, gate_probs, gate_weight, up_weight, down_weight):
    expert_count = lax.axis_size("expert")
    group_size = lax.axis_size("dp")
    token_count = activations.shape[0]
    feature_width = activations.shape[1]
    routes_each = expert_ids.shape[1]
    capacity = max(2, 3 * token_count * routes_each // expert_count)
    slab_rows = expert_count * capacity
    group_rows = slab_rows * group_size
    w_gate = gate_weight[0]
    w_up = up_weight[0]
    w_down = down_weight[0]
    hidden = w_gate.shape[1]
    routes = expert_ids[:, 0]
    onehot = (routes[:, None] == jnp.arange(expert_count, dtype=jnp.int32)[None, :]).astype(
        jnp.int32
    )
    earlier = jnp.cumsum(onehot, axis=0) - onehot
    slot_index = jnp.sum(earlier * onehot, axis=1)
    target = routes * capacity + slot_index
    source = (
        jnp.zeros((slab_rows,), jnp.int32).at[target].set(jnp.arange(token_count, dtype=jnp.int32))
    )
    filled = jnp.zeros((slab_rows,), jnp.bool_).at[target].set(True)
    slot_probs = jnp.where(filled, gate_probs[source, 0], 0)
    send_tokens = jnp.where(filled[:, None], activations[source], 0)
    send_grads = jnp.where(filled[:, None], out_grad[source], 0)
    arrived_tokens, arrived_grads, arrived_probs = (
        lax.all_to_all(
            send_tokens.reshape(expert_count, capacity, feature_width),
            "expert",
            split_axis=0,
            concat_axis=0,
            tiled=True,
        ),
        lax.all_to_all(
            send_grads.reshape(expert_count, capacity, feature_width),
            "expert",
            split_axis=0,
            concat_axis=0,
            tiled=True,
        ),
        lax.all_to_all(
            slot_probs.reshape(expert_count, capacity),
            "expert",
            split_axis=0,
            concat_axis=0,
            tiled=True,
        ),
    )
    own_tokens = arrived_tokens.reshape(slab_rows, feature_width)
    own_grads = arrived_grads.reshape(slab_rows, feature_width)
    spread_probs = jnp.broadcast_to(arrived_probs.reshape(slab_rows, 1), (slab_rows, group_size))
    group_tokens, group_grads, group_spread = (
        lax.all_to_all(own_tokens, "dp", split_axis=1, concat_axis=0, tiled=True),
        lax.all_to_all(own_grads, "dp", split_axis=1, concat_axis=0, tiled=True),
        lax.all_to_all(spread_probs, "dp", split_axis=1, concat_axis=0, tiled=True),
    )
    group_probs = group_spread.reshape(group_rows)
    first_row = lax.axis_index("dp") * slab_rows
    own_probs = lax.dynamic_slice_in_dim(group_probs, first_row, slab_rows, 0)
    row_tokens = group_tokens
    row_grads = group_grads
    own_sums = lax.psum_scatter(
        jnp.concatenate(
            [
                jnp.dot(row_tokens, w_gate, preferred_element_type=jnp.float32),
                jnp.dot(row_tokens, w_up, preferred_element_type=jnp.float32),
                jnp.dot(row_grads, w_down, preferred_element_type=jnp.float32),
            ],
            axis=1,
        ).astype(jnp.bfloat16),
        "dp",
        scatter_dimension=0,
        tiled=True,
    ).astype(jnp.float32)
    own_hidden, gate_rows, up_rows = activate(own_sums, own_probs, hidden)
    hidden_rows = lax.all_gather(own_hidden, "dp", axis=0, tiled=True)
    accumulate_gate_rows = lax.all_gather(gate_rows, "dp", axis=0, tiled=True)
    accumulate_up_rows = lax.all_gather(up_rows, "dp", axis=0, tiled=True)
    prob_rows = lax.all_gather(own_probs, "dp", axis=0, tiled=True)
    row_tokens = group_tokens
    row_grads = group_grads
    scaled = (prob_rows.astype(jnp.float32)[:, None] * hidden_rows.astype(jnp.float32)).astype(
        jnp.bfloat16
    )
    new_gate = jnp.einsum(
        "rd,rf->df", row_tokens, accumulate_gate_rows, preferred_element_type=jnp.float32
    )
    new_up = jnp.einsum(
        "rd,rf->df", row_tokens, accumulate_up_rows, preferred_element_type=jnp.float32
    )
    new_down = jnp.einsum("rd,rf->df", row_grads, scaled, preferred_element_type=jnp.float32)
    back_rows = jnp.einsum(
        "rf,df->rd", accumulate_gate_rows, w_gate, preferred_element_type=jnp.float32
    )
    back_rows = back_rows + jnp.einsum(
        "rf,df->rd", accumulate_up_rows, w_up, preferred_element_type=jnp.float32
    )
    output_rows = jnp.einsum("rf,df->rd", hidden_rows, w_down, preferred_element_type=jnp.float32)
    inner_terms = jnp.sum(row_grads.astype(jnp.float32) * output_rows, axis=1)
    prob_terms = lax.psum_scatter(inner_terms, "dp", scatter_dimension=0, tiled=True)
    prob_rounded = prob_terms.astype(jnp.bfloat16)
    back_rounded = back_rows.astype(jnp.bfloat16)
    returned_rows = lax.all_to_all(back_rounded, "dp", split_axis=0, concat_axis=1, tiled=True)
    final_rows, final_probs = (
        lax.all_to_all(
            returned_rows.reshape(expert_count, capacity, feature_width),
            "expert",
            split_axis=0,
            concat_axis=0,
            tiled=True,
        ),
        lax.all_to_all(
            prob_rounded.reshape(expert_count, capacity),
            "expert",
            split_axis=0,
            concat_axis=0,
            tiled=True,
        ),
    )
    input_delta = final_rows.reshape(slab_rows, feature_width)[target]
    prob_delta = final_probs.reshape(slab_rows)[target][:, None]
    return (
        input_delta,
        prob_delta,
        new_gate.astype(jnp.bfloat16)[None],
        new_up.astype(jnp.bfloat16)[None],
        new_down.astype(jnp.bfloat16)[None],
    )


def solution(mesh):
    return jax.shard_map(
        on_device,
        mesh=mesh,
        in_specs=(
            P(("expert", "dp"), None),
            P(("expert", "dp"), None),
            P(("expert", "dp"), None),
            P(("expert", "dp"), None),
            P("expert", "dp", None),
            P("expert", "dp", None),
            P("expert", "dp", None),
        ),
        out_specs=(
            P(("expert", "dp"), None),
            P(("expert", "dp"), None),
            P("expert", "dp", None),
            P("expert", "dp", None),
            P("expert", "dp", None),
        ),
        check_vma=False,
    )
```

profile of v0, /device:TPU:52, one launch (start us, length us, event | category | flops | bytes accessed | tf_op | source)
XLA Modules:
  0.0 543.7 jit_solution(1405030936872476756)
XLA Ops:
  14.6 5.5 %gather.21 = bf16[64,6,3584]{2,1,0:T(8,128)(2,1)} reshape(bf16[384,3584]{1,0:T(8,128)(2,1)} %gather_fusion.1) | data formatting | bytes 5505024 | tf_op jit(solution)/shard_map/gather | solution.py:46
  23.9 5.4 gather.23
  35.3 54.0 %all_to_all.102 = bf16[64,6,3584]{2,1,0:T(8,128)(2,1)} all-to-all(bf16[64,6,3584]{2,1,0:T(8,128)(2,1)S(1)} %get-tuple-element.10), channel_id=1, replica_groups=mesh['expert'=64,'dp'=2] {'expert'}, dimensions={0} | all-to-all | bytes 5505024 | tf_op jit(solution)/shard_map/all_to_all | solution.py:49
  89.2 10.3 %all-to-all-start.4 = ((bf16[64,6,3584]{2,1,0:T(8,128)(2,1)}), bf16[64,6,3584]{2,1,0:T(8,128)(2,1)}, u32[]{:S(2)}, u32[]{:S(2)}) async-start(bf16[64,6,3584]{2,1,0:T(8,128)(2,1)} %get-tuple-element.11), calls=%async_computation.4 | async-start | bytes 7340032 | tf_op jit(solution)/shard_map/all_to_all | solution.py:56
  99.6 7.3 %all_to_all.76 = bf16[384,2,1792]{2,1,0:T(2,128)(2,1)} reshape(bf16[64,6,3584]{2,1,0:T(8,128)(2,1)} %all_to_all.102) | data formatting | bytes 5505024 | tf_op jit(solution)/shard_map/all_to_all | solution.py:75
  110.4 37.4 %all-to-all-done.4 = bf16[64,6,3584]{2,1,0:T(8,128)(2,1)} async-done(((bf16[64,6,3584]{2,1,0:T(8,128)(2,1)}), bf16[64,6,3584]{2,1,0:T(8,128)(2,1)}, u32[]{:S(2)}, u32[]{:S(2)}) %all-to-all-start.4) | async-done | bytes 2752544 | tf_op jit(solution)/shard_map/all_to_all | solution.py:56
  147.9 5.2 all-to-all-start.3
  153.0 7.3 %all_to_all.81 = bf16[384,2,1792]{2,1,0:T(2,128)(2,1)} reshape(bf16[64,6,3584]{2,1,0:T(8,128)(2,1)} %all-to-all-done.4) | data formatting | bytes 5505024 | tf_op jit(solution)/shard_map/all_to_all | solution.py:76
  163.9 22.1 %all-to-all-done.3 = bf16[384,2,1792]{2,0,1:T(8,128)(2,1)} async-done(((bf16[384,2,1792]{2,0,1:T(8,128)(2,1)}), bf16[384,2,1792]{2,0,1:T(8,128)(2,1)}, u32[]{:S(2)}, u32[]{:S(2)}) %all-to-all-start.3) | async-done | bytes 2752544 | tf_op jit(solution)/shard_map/all_to_all | solution.py:75
  191.4 6.0 %fusion.16 = bf16[768,1024]{1,0:T(8,128)(2,1)S(1)} fusion(bf16[768,1792]{1,0:T(8,128)(2,1)} %bitcast.5, bf16[1,1792,1024]{2,1,0:T(8,128)(2,1)} %param.11), kind=kOutput, calls=%fused_computation.30 | convolution fusion | flops 2819358720 | bytes 7995392 | tf_op jit(solution)/shard_map/dot_general | solution.py:87
  197.4 5.9 %fusion.19 = bf16[768,1024]{1,0:T(8,128)(2,1)} fusion(bf16[768,1792]{1,0:T(8,128)(2,1)} %bitcast.5, bf16[1,1792,1024]{2,1,0:T(8,128)(2,1)S(1)} %copy-done.5), kind=kOutput, calls=%fused_computation.31 | convolution fusion | flops 2819358720 | bytes 7995392 | tf_op jit(solution)/shard_map/dot_general | solution.py:88
  203.3 19.9 %all-to-all-done.5 = bf16[384,2,1792]{2,0,1:T(8,128)(2,1)} async-done(((bf16[384,2,1792]{2,0,1:T(8,128)(2,1)}), bf16[384,2,1792]{2,0,1:T(8,128)(2,1)}, u32[]{:S(2)}, u32[]{:S(2)}) %all-to-all-start.5) | async-done | bytes 2752544 | tf_op jit(solution)/shard_map/all_to_all | solution.py:76
  223.3 6.0 %fusion.22 = bf16[768,1024]{1,0:T(8,128)(2,1)S(1)} fusion(bf16[768,1792]{1,0:T(8,128)(2,1)} %bitcast.10, bf16[1,1792,1024]{2,1,0:T(8,128)(2,1)} %param.13), kind=kOutput, calls=%fused_computation.32 | convolution fusion | flops 2819358720 | bytes 7995392 | tf_op jit(solution)/shard_map/dot_general | solution.py:89
  235.1 13.5 %all_to_all.103 = bf16[64,1,6]{2,1,0:T(2,128)(2,1)S(1)} all-to-all(bf16[64,1,6]{2,1,0:T(2,128)(2,1)S(1)} %all_to_all.91), channel_id=1, replica_groups=mesh['expert'=64,'dp'=2] {'expert'}, dimensions={0} | all-to-all | bytes 1536 | tf_op jit(solution)/shard_map/all_to_all | solution.py:63
  257.9 36.4 %reduce-scatter.2.cloned.1.call-done = bf16[384,3072]{1,0:T(8,128)(2,1)} async-done(((bf16[768,3072]{1,0:T(8,128)(2,1)}), bf16[384,3072]{1,0:T(8,128)(2,1)}) %reduce-scatter.2.cloned.1.call-update) | async-done | bytes 2359312 | tf_op jit(solution)/shard_map/reduce_scatter | solution.py:84
  300.4 29.5 %all-gather.7.cloned.1.call-done = bf16[768,1024]{1,0:T(8,128)(2,1)} async-done(((bf16[384,1024]{1,0:T(8,128)(2,1)}), bf16[768,1024]{1,0:T(8,128)(2,1)}) %all-gather.7.cloned.1.call-update) | async-done | bytes 1572880 | tf_op jit(solution)/shard_map/all_gather | solution.py:100
  329.9 8.0 %fusion.3 = f32[768,1792]{1,0:T(8,128)} fusion(bf16[768,1024]{1,0:T(8,128)(2,1)} %all-gather.7.cloned.1.call-done, bf16[1,1792,1024]{2,1,0:T(8,128)(2,1)} %param.12), kind=kOutput, calls=%fused_computation.16 | convolution fusion | flops 2818572288 | bytes 10747904 | tf_op jit(solution)/shard_map/rf,df->rd/dot_general | solution.py:117
  337.9 25.1 %all-gather.5.cloned.1.call-done = bf16[768,1024]{1,0:T(8,128)(2,1)} async-done(((bf16[384,1024]{1,0:T(8,128)(2,1)}), bf16[768,1024]{1,0:T(8,128)(2,1)}) %all-gather.5.cloned.1.call-update) | async-done | bytes 1572880 | tf_op jit(solution)/shard_map/all_gather | solution.py:99
  363.0 8.7 %add_convert_fusion = bf16[768,1792]{1,0:T(8,128)(2,1)} fusion(f32[768,1792]{1,0:T(8,128)} %fusion.3, bf16[768,1024]{1,0:T(8,128)(2,1)} %all-gather.5.cloned.1.call-done, bf16[1,1792,1024]{2,1,0:T(8,128)(2,1)} %param.11), kind=kOutput, calls=%fused_computation.8 | convolution fusion | flops 2821324800 | bytes 13500416 | tf_op jit(solution)/shard_map/rf,df->rd/dot_general | solution.py:114
  371.7 5.2 all-to-all-start.6
  378.2 33.9 %all-gather.9.cloned.1.call-done = bf16[768,1024]{1,0:T(8,128)(2,1)} async-done(((bf16[384,1024]{1,0:T(8,128)(2,1)}), bf16[768,1024]{1,0:T(8,128)(2,1)}) %all-gather.9.cloned.1.call-update) | async-done | bytes 1572880 | tf_op jit(solution)/shard_map/all_gather | solution.py:98
  412.1 6.5 %multiply_reduce_fusion = f32[768]{0:T(1024)S(1)} fusion(bf16[768,1792]{1,0:T(8,128)(2,1)} %bitcast.10, bf16[768,1024]{1,0:T(8,128)(2,1)} %all-gather.9.cloned.1.call-done, bf16[1,1792,1024]{2,1,0:T(8,128)(2,1)} %param.13), kind=kOutput, calls=%fused_computation.7 | convolution fusion | flops 2822700288 | bytes 7998464 | tf_op jit(solution)/shard_map/rf,df->rd/dot_general | solution.py:120
  418.6 6.7 %all-reduce.1 = bf16[768]{0:T(1024)(128)(2,1)S(1)} all-reduce(f32[768]{0:T(1024)S(1)} %multiply_reduce_fusion), channel_id=3, replica_groups=mesh['expert'=64,'dp'=2] {'dp'}, use_global_device_ids=true, to_apply=%region_6.7.clone | all-reduce | flops 768 | bytes 4608
  426.1 10.6 %all-to-all-start.8 = ((bf16[64,1,6]{2,1,0:T(2,128)(2,1)}), bf16[64,1,6]{2,1,0:T(2,128)(2,1)S(1)}, u32[]{:S(2)}, u32[]{:S(2)}) async-start(bf16[64,1,6]{2,1,0:T(2,128)(2,1)} %all_to_all.92), calls=%async_computation.9 | async-start | bytes 65536 | tf_op jit(solution)/shard_map/all_to_all | solution.py:134
  436.8 6.1 %copy.18 = bf16[384,2,1792]{2,1,0:T(2,128)(2,1)} copy(bf16[384,2,1792]{2,0,1:T(8,128)(2,1)} %bitcast.13) | data formatting | bytes 5505024 | tf_op jit(solution)/shard_map/all_to_all | solution.py:125
  442.9 7.6 %reshape.76 = bf16[64,6,3584]{2,1,0:T(8,128)(2,1)} reshape(bf16[384,2,1792]{2,1,0:T(2,128)(2,1)} %copy.18) | data formatting | bytes 5505024 | tf_op jit(solution)/shard_map/reshape | solution.py:128
  450.5 10.6 %all-to-all-start.7 = ((bf16[64,6,3584]{2,1,0:T(8,128)(2,1)}), bf16[64,6,3584]{2,1,0:T(8,128)(2,1)}, u32[]{:S(2)}, u32[]{:S(2)}) async-start(bf16[64,6,3584]{2,1,0:T(8,128)(2,1)} %reshape.76), calls=%async_computation.8 | async-start | bytes 7340032 | tf_op jit(solution)/shard_map/all_to_all | solution.py:127
  461.2 43.8 %all-gather = bf16[2,1,384]{2,1,0:T(2,128)(2,1)S(1)} all-gather(bf16[1,1,384]{2,1,0:T(2,128)(2,1)S(1)} %reshape.141), channel_id=1, replica_groups=mesh['expert'=64,'dp'=2] {'dp'}, dimensions={0}, use_global_device_ids=true | all-gather | bytes 2304 | tf_op jit(solution)/shard_map/all_gather | solution.py:101
  505.1 6.4 %fusion.12 = bf16[1,1792,1024]{2,1,0:T(8,128)(2,1)} fusion(bf16[768,1792]{1,0:T(8,128)(2,1)} %bitcast.5, bf16[768,1024]{1,0:T(8,128)(2,1)S(1)} %copy-done.6), kind=kOutput, calls=%fused_computation.27 | convolution fusion | flops 2820407296 | bytes 7995392 | tf_op jit(solution)/shard_map/rd,rf->df/dot_general | solution.py:110
  511.5 6.4 %fusion.11 = bf16[1,1792,1024]{2,1,0:T(8,128)(2,1)} fusion(bf16[768,1792]{1,0:T(8,128)(2,1)} %bitcast.5, bf16[768,1024]{1,0:T(8,128)(2,1)S(1)} %copy-done.7), kind=kOutput, calls=%fused_computation.26 | convolution fusion | flops 2820407296 | bytes 7995392 | tf_op jit(solution)/shard_map/rd,rf->df/dot_general | solution.py:107
  517.9 6.4 %fusion.13 = bf16[1,1792,1024]{2,1,0:T(8,128)(2,1)} fusion(bf16[768,1792]{1,0:T(8,128)(2,1)} %bitcast.10, bf16[768,1024]{1,0:T(8,128)(2,1)S(1)} %copy-done.8, f32[768]{0:T(1024)S(1)} %reshape.143), kind=kOutput, calls=%fused_computation.28 | convolution fusion | flops 2822766592 | bytes 7998464 | tf_op jit(solution)/shard_map/rd,rf->df/dot_general | solution.py:113
  526.3 5.6 %reshape.77 = bf16[384,3584]{1,0:T(8,128)(2,1)} reshape(bf16[64,6,3584]{2,1,0:T(8,128)(2,1)} %all-to-all-done.7) | data formatting | bytes 5505024 | tf_op jit(solution)/shard_map/reshape | solution.py:142
  (77 shorter events, 59.4 us)
Async XLA Ops:
  7.2 3.5 copy-start
  14.6 5.5 %copy-start.3 = (bf16[128,3584]{1,0:T(8,128)(2,1)S(1)}, bf16[128,3584]{1,0:T(8,128)(2,1)}, u32[]{:S(2)}) copy-start(bf16[128,3584]{1,0:T(8,128)(2,1)} %param.8) | copy-start | bytes 2752516
  89.2 58.7 %all-to-all-start.4 = ((bf16[64,6,3584]{2,1,0:T(8,128)(2,1)}), bf16[64,6,3584]{2,1,0:T(8,128)(2,1)}, u32[]{:S(2)}, u32[]{:S(2)}) async-start(bf16[64,6,3584]{2,1,0:T(8,128)(2,1)} %get-tuple-element.11), calls=%async_computation.4 | async-start | bytes 7340032 | tf_op jit(solution)/shard_map/all_to_all | solution.py:56
  147.9 38.1 %all-to-all-start.3 = ((bf16[384,2,1792]{2,0,1:T(8,128)(2,1)}), bf16[384,2,1792]{2,0,1:T(8,128)(2,1)}, u32[]{:S(2)}, u32[]{:S(2)}) async-start(bf16[384,2,1792]{2,0,1:T(8,128)(2,1)} %copy.16), calls=%async_computation.3 | async-start | bytes 5505024 | tf_op jit(solution)/shard_map/all_to_all | solution.py:75
  186.0 37.3 %all-to-all-start.5 = ((bf16[384,2,1792]{2,0,1:T(8,128)(2,1)}), bf16[384,2,1792]{2,0,1:T(8,128)(2,1)}, u32[]{:S(2)}, u32[]{:S(2)}) async-start(bf16[384,2,1792]{2,0,1:T(8,128)(2,1)} %copy.17), calls=%async_computation.5 | async-start | bytes 5505024 | tf_op jit(solution)/shard_map/all_to_all | solution.py:76
  191.1 103.3 %reduce-scatter.2.cloned.1.call-start = ((), (), s32[]{:S(2)}) async-start(), calls=%async_computation.10 | async-start | bytes 7077888 | tf_op jit(solution)/shard_map/reduce_scatter | solution.py:84
  191.4 6.0 %copy-start.5 = (bf16[1,1792,1024]{2,1,0:T(8,128)(2,1)S(1)}, bf16[1,1792,1024]{2,1,0:T(8,128)(2,1)}, u32[]{:S(2)}) copy-start(bf16[1,1792,1024]{2,1,0:T(8,128)(2,1)} %param.12) | copy-start | bytes 11010052
  223.3 6.0 %copy-start.4 = (bf16[768,1024]{1,0:T(8,128)(2,1)S(1)}, bf16[768,1024]{1,0:T(8,128)(2,1)}, u32[]{:S(2)}) copy-start(bf16[768,1024]{1,0:T(8,128)(2,1)} %fusion.19) | copy-start | bytes 4718596
  231.6 0.7 copy-start.2
  250.7 7.0 %all-to-all-start.1 = ((bf16[2,2,192]{2,1,0:T(2,128)(2,1)}), bf16[2,2,192]{2,1,0:T(2,128)(2,1)S(1)}, u32[]{:S(2)}, u32[]{:S(2)}) async-start(bf16[2,2,192]{2,1,0:T(2,128)(2,1)} %reshape.153), calls=%async_computation.1 | async-start | bytes 4096 | tf_op jit(solution)/shard_map/all_to_all | solution.py:77
  253.9 76.0 %all-gather.7.cloned.1.call-start = ((), (), s32[]{:S(2)}) async-start(), calls=%async_computation.12 | async-start | bytes 2359296 | tf_op jit(solution)/shard_map/all_gather | solution.py:100
  299.1 63.9 %all-gather.5.cloned.1.call-start = ((), (), s32[]{:S(2)}) async-start(), calls=%async_computation.11 | async-start | bytes 2359296 | tf_op jit(solution)/shard_map/all_gather | solution.py:99
  299.8 112.3 %all-gather.9.cloned.1.call-start = ((), (), s32[]{:S(2)}) async-start(), calls=%async_computation.13 | async-start | bytes 2359296 | tf_op jit(solution)/shard_map/all_gather | solution.py:98
  371.7 5.2 copy-start.9
  371.7 54.4 %all-to-all-start.6 = ((bf16[2,384,1792]{2,1,0:T(8,128)(2,1)}), bf16[2,384,1792]{2,1,0:T(8,128)(2,1)}, u32[]{:S(2)}, u32[]{:S(2)}) async-start(bf16[2,384,1792]{2,1,0:T(8,128)(2,1)} %bitcast.63), calls=%async_computation.7 | async-start | bytes 5505024 | tf_op jit(solution)/shard_map/all_to_all | solution.py:125
  426.1 24.4 %all-to-all-start.8 = ((bf16[64,1,6]{2,1,0:T(2,128)(2,1)}), bf16[64,1,6]{2,1,0:T(2,128)(2,1)S(1)}, u32[]{:S(2)}, u32[]{:S(2)}) async-start(bf16[64,1,6]{2,1,0:T(2,128)(2,1)} %all_to_all.92), calls=%async_computation.9 | async-start | bytes 65536 | tf_op jit(solution)/shard_map/all_to_all | solution.py:134
  450.5 54.5 %copy-start.6 = (bf16[768,1024]{1,0:T(8,128)(2,1)S(1)}, bf16[768,1024]{1,0:T(8,128)(2,1)}, u32[]{:S(2)}) copy-start(bf16[768,1024]{1,0:T(8,128)(2,1)} %all-gather.7.cloned.1.call-done) | copy-start | bytes 4718596
  450.5 75.8 %all-to-all-start.7 = ((bf16[64,6,3584]{2,1,0:T(8,128)(2,1)}), bf16[64,6,3584]{2,1,0:T(8,128)(2,1)}, u32[]{:S(2)}, u32[]{:S(2)}) async-start(bf16[64,6,3584]{2,1,0:T(8,128)(2,1)} %reshape.76), calls=%async_computation.8 | async-start | bytes 7340032 | tf_op jit(solution)/shard_map/all_to_all | solution.py:127
  505.0 6.4 %copy-start.7 = (bf16[768,1024]{1,0:T(8,128)(2,1)S(1)}, bf16[768,1024]{1,0:T(8,128)(2,1)}, u32[]{:S(2)}) copy-start(bf16[768,1024]{1,0:T(8,128)(2,1)} %all-gather.5.cloned.1.call-done) | copy-start | bytes 4718596
  511.5 6.4 %copy-start.8 = (bf16[768,1024]{1,0:T(8,128)(2,1)S(1)}, bf16[768,1024]{1,0:T(8,128)(2,1)}, u32[]{:S(2)}) copy-start(bf16[768,1024]{1,0:T(8,128)(2,1)} %all-gather.9.cloned.1.call-done) | copy-start | bytes 4718596
  526.3 10.7 %copy-start.1 = (bf16[128,3584]{1,0:T(8,128)(2,1)S(1)}, bf16[128,3584]{1,0:T(8,128)(2,1)}, u32[]{:S(2)}) copy-start(bf16[128,3584]{1,0:T(8,128)(2,1)} %param.7) | copy-start | bytes 2752516
Sparse Core Ops, SparseCore 0:
  231.7 62.5 reduce-scatter.1
  299.2 30.6 all-gather.6
  332.2 30.6 all-gather.4
  365.1 46.8 all-gather.8
where the time goes:
time: 553 us; the launch traced here: 544 us
  waiting for transfers between devices  209 us (38%)
  blocking collectives  118 us (21%)
  local copies, waits for them, and re-layouts  75.1 us (14%)
  matrix products  60.3 us (11%)
  starting transfers between devices  51.2 us (9%)
  other arithmetic  15.3 us (3%)
  between operations  14.9 us (3%)
    all_to_all x1, blocking collectives, on_device(): lax.all_to_all(send_tokens.reshape(expert_count, capacity, feature_width)...  54 us
    all_gather x1, blocking collectives, on_device(): prob_rows = lax.all_gather(own_probs, 'dp', axis=0, tiled=True)  43.8 us
    all_to_all x1, waiting for transfers between devices, on_device(): lax.all_to_all(send_grads.reshape(expert_count, capacity, feature_width),...  37.4 us
    reduce_scatter x1, waiting for transfers between devices, on_device(): lax.psum_scatter(jnp.concatenate([jnp.dot(row_tokens, w_gate, preferred_e...  36.4 us
    all_gather x1, waiting for transfers between devices, on_device(): hidden_rows = lax.all_gather(own_hidden, 'dp', axis=0, tiled=True)  33.9 us
    all_gather x1, waiting for transfers between devices, on_device(): accumulate_up_rows = lax.all_gather(up_rows, 'dp', axis=0, tiled=True)  29.5 us
    all_gather x1, waiting for transfers between devices, on_device(): accumulate_gate_rows = lax.all_gather(gate_rows, 'dp', axis=0, tiled=True)  25.1 us
    all_to_all x1, waiting for transfers between devices, on_device(): lax.all_to_all(own_tokens, 'dp', split_axis=1, concat_axis=0, tiled=True)  22.1 us
  transfers between devices with their start and end apart: 11, of which 8 were waited for; matrix products, arithmetic and copies ran while one was open for 15% of the time, Pallas kernels for 0%

commit v1 on v0

--- a/solution.py
+++ b/solution.py
@@ -2,6 +2,10 @@
 import jax.numpy as jnp
 from jax import lax
 from jax.sharding import PartitionSpec as P
+
+_order_set = lambda mine, mesh_ax, dim_at: jnp.concatenate(
+    lax.all_to_all(jnp.stack([mine for _ in range(lax.axis_size(mesh_ax))]), mesh_ax, 0, 0), dim_at
+)
 
 
 def activate(summed, prob_rows, hidden):
@@ -96,7 +100,7 @@
     ).astype(jnp.float32)
     own_hidden, gate_rows, up_rows = activate(own_sums, own_probs, hidden)
     hidden_rows = lax.all_gather(own_hidden, "dp", axis=0, tiled=True)
-    accumulate_gate_rows = lax.all_gather(gate_rows, "dp", axis=0, tiled=True)
+    accumulate_gate_rows = _order_set(gate_rows, "dp", 0)
     accumulate_up_rows = lax.all_gather(up_rows, "dp", axis=0, tiled=True)
     prob_rows = lax.all_gather(own_probs, "dp", axis=0, tiled=True)
     row_tokens = group_tokens

time: 553 us -> 529 us (0.957)
  waiting for transfers between devices: 209 us -> 169 us
  local copies, waits for them, and re-layouts: 75.1 us -> 84.6 us
  blocking collectives: 118 us -> 125 us
    all_gather x1 -> x0, waiting for transfers between devices: 25.1 us -> none  [on_device(): accumulate_gate_rows = lax.all_gather(gate_rows, 'dp', axis=0, tiled=True)]
    all_gather x1, waiting for transfers between devices: 33.9 us -> 20.8 us  [on_device(): hidden_rows = lax.all_gather(own_hidden, 'dp', axis=0, tiled=True)]
    all_to_all x2 -> x3, local copies, waits for them, and re-layouts: 10.9 us -> 20.3 us  [on_device(): lax.all_to_all(own_tokens, 'dp', split_axis=1, concat_axis=0, tiled=True)]
    unnamed x1, blocking collectives: 6.72 us -> 13.4 us
    all_gather x1, waiting for transfers between devices: 29.5 us -> 35.8 us  [on_device(): accumulate_up_rows = lax.all_gather(up_rows, 'dp', axis=0, tiled=True)]
  transfers between devices with their start and end apart: 11 -> 11, of which waited for: 8 -> 7; matrix products, arithmetic and copies ran while one was open for 15% -> 17% of each run, Pallas kernels for 0% -> 0%
where the time goes in v1:
time: 529 us; the launch traced here: 519 us
  waiting for transfers between devices  169 us (32%)
  blocking collectives  125 us (24%)
  local copies, waits for them, and re-layouts  84.6 us (16%)
  matrix products  55.1 us (10%)
  starting transfers between devices  54.7 us (10%)
  other arithmetic  16.3 us (3%)
  between operations  14.9 us (3%)
    all_to_all x1, blocking collectives, on_device(): lax.all_to_all(send_tokens.reshape(expert_count, capacity, feature_width)...  54 us
    all_gather x1, blocking collectives, on_device(): prob_rows = lax.all_gather(own_probs, 'dp', axis=0, tiled=True)  43.8 us
    reduce_scatter x1, waiting for transfers between devices, on_device(): lax.psum_scatter(jnp.concatenate([jnp.dot(row_tokens, w_gate, preferred_e...  36.4 us
    all_gather x1, waiting for transfers between devices, on_device(): accumulate_up_rows = lax.all_gather(up_rows, 'dp', axis=0, tiled=True)  35.8 us
    all_to_all x1, waiting for transfers between devices, on_device(): lax.all_to_all(send_grads.reshape(expert_count, capacity, feature_width),...  32.5 us
    all_to_all x1, waiting for transfers between devices, on_device(): lax.all_to_all(own_tokens, 'dp', split_axis=1, concat_axis=0, tiled=True)  22.1 us
    all_gather x1, waiting for transfers between devices, on_device(): hidden_rows = lax.all_gather(own_hidden, 'dp', axis=0, tiled=True)  20.8 us
    all_to_all x3, local copies, waits for them, and re-layouts, on_device(): lax.all_to_all(own_tokens, 'dp', split_axis=1, concat_axis=0, tiled=True)  20.3 us
  transfers between devices with their start and end apart: 11, of which 7 were waited for; matrix products, arithmetic and copies ran while one was open for 17% of the time, Pallas kernels for 0%

profile of v1, /device:TPU:52, one launch (start us, length us, event | category | flops | bytes accessed | tf_op | source)
XLA Modules:
  0.0 519.3 jit_solution(1841694939668939408)
XLA Ops:
  14.6 5.5 %gather.21 = bf16[64,6,3584]{2,1,0:T(8,128)(2,1)} reshape(bf16[384,3584]{1,0:T(8,128)(2,1)} %gather_fusion.1) | data formatting | bytes 5505024 | tf_op jit(solution)/shard_map/gather | solution.py:50
  23.9 5.4 %gather.23 = bf16[64,6,3584]{2,1,0:T(8,128)(2,1)} reshape(bf16[384,3584]{1,0:T(8,128)(2,1)} %gather_fusion.2) | data formatting | bytes 5505024 | tf_op jit(solution)/shard_map/gather | solution.py:51
  35.3 54.0 %all_to_all.107 = bf16[64,6,3584]{2,1,0:T(8,128)(2,1)} all-to-all(bf16[64,6,3584]{2,1,0:T(8,128)(2,1)S(1)} %get-tuple-element.10), channel_id=1, replica_groups=mesh['expert'=64,'dp'=2] {'expert'}, dimensions={0} | all-to-all | bytes 5505024 | tf_op jit(solution)/shard_map/all_to_all | solution.py:53
  89.2 10.3 %all-to-all-start.4 = ((bf16[64,6,3584]{2,1,0:T(8,128)(2,1)}), bf16[64,6,3584]{2,1,0:T(8,128)(2,1)}, u32[]{:S(2)}, u32[]{:S(2)}) async-start(bf16[64,6,3584]{2,1,0:T(8,128)(2,1)} %get-tuple-element.11), calls=%async_computation.4 | async-start | bytes 7340032 | tf_op jit(solution)/shard_map/all_to_all | solution.py:60
  99.6 7.3 %all_to_all.79 = bf16[384,2,1792]{2,1,0:T(2,128)(2,1)} reshape(bf16[64,6,3584]{2,1,0:T(8,128)(2,1)} %all_to_all.107) | data formatting | bytes 5505024 | tf_op jit(solution)/shard_map/all_to_all | solution.py:79
  106.8 8.6 %copy.19 = bf16[384,2,1792]{0,2,1:T(8,128)(2,1)} copy(bf16[384,2,1792]{2,1,0:T(2,128)(2,1)} %all_to_all.79) | data formatting | bytes 5505024 | tf_op jit(solution)/shard_map/all_to_all | solution.py:79
  115.4 32.5 %all-to-all-done.4 = bf16[64,6,3584]{2,1,0:T(8,128)(2,1)} async-done(((bf16[64,6,3584]{2,1,0:T(8,128)(2,1)}), bf16[64,6,3584]{2,1,0:T(8,128)(2,1)}, u32[]{:S(2)}, u32[]{:S(2)}) %all-to-all-start.4) | async-done | bytes 2752544 | tf_op jit(solution)/shard_map/all_to_all | solution.py:60
  147.9 5.1 all-to-all-start.3
  152.9 7.3 %all_to_all.84 = bf16[384,2,1792]{2,1,0:T(2,128)(2,1)} reshape(bf16[64,6,3584]{2,1,0:T(8,128)(2,1)} %all-to-all-done.4) | data formatting | bytes 5505024 | tf_op jit(solution)/shard_map/all_to_all | solution.py:80
  163.8 22.1 %all-to-all-done.3 = bf16[384,2,1792]{0,2,1:T(8,128)(2,1)} async-done(((bf16[384,2,1792]{0,2,1:T(8,128)(2,1)}), bf16[384,2,1792]{0,2,1:T(8,128)(2,1)}, u32[]{:S(2)}, u32[]{:S(2)}) %all-to-all-start.3) | async-done | bytes 2752544 | tf_op jit(solution)/shard_map/all_to_all | solution.py:79
  185.9 5.2 all-to-all-start.5
  195.9 6.0 %fusion.16 = bf16[768,1024]{1,0:T(8,128)(2,1)S(1)} fusion(bf16[768,1792]{1,0:T(8,128)(2,1)} %bitcast.70, bf16[1,1792,1024]{2,1,0:T(8,128)(2,1)} %param.11), kind=kOutput, calls=%fused_computation.30 | convolution fusion | flops 2819358720 | bytes 7995392 | tf_op jit(solution)/shard_map/dot_general | solution.py:91
  206.0 17.2 %all-to-all-done.5 = bf16[384,2,1792]{2,0,1:T(8,128)(2,1)} async-done(((bf16[384,2,1792]{2,0,1:T(8,128)(2,1)}), bf16[384,2,1792]{2,0,1:T(8,128)(2,1)}, u32[]{:S(2)}, u32[]{:S(2)}) %all-to-all-start.5) | async-done | bytes 2752544 | tf_op jit(solution)/shard_map/all_to_all | solution.py:80
  223.3 6.0 %fusion.22 = bf16[768,1024]{1,0:T(8,128)(2,1)S(1)} fusion(bf16[768,1792]{1,0:T(8,128)(2,1)} %bitcast.9, bf16[1,1792,1024]{2,1,0:T(8,128)(2,1)} %param.13), kind=kOutput, calls=%fused_computation.32 | convolution fusion | flops 2819358720 | bytes 7995392 | tf_op jit(solution)/shard_map/dot_general | solution.py:93
  235.1 13.5 %all_to_all.108 = bf16[64,1,6]{2,1,0:T(2,128)(2,1)S(1)} all-to-all(bf16[64,1,6]{2,1,0:T(2,128)(2,1)S(1)} %all_to_all.95), channel_id=1, replica_groups=mesh['expert'=64,'dp'=2] {'expert'}, dimensions={0} | all-to-all | bytes 1536 | tf_op jit(solution)/shard_map/all_to_all | solution.py:67
  257.9 36.4 %reduce-scatter.2.cloned.1.call-done = bf16[384,3072]{1,0:T(8,128)(2,1)} async-done(((bf16[768,3072]{1,0:T(8,128)(2,1)}), bf16[384,3072]{1,0:T(8,128)(2,1)}) %reduce-scatter.2.cloned.1.call-update) | async-done | bytes 2359312 | tf_op jit(solution)/shard_map/reduce_scatter | solution.py:88
  304.6 35.8 %all-gather.4.cloned.1.call-done = bf16[768,1024]{1,0:T(8,128)(2,1)} async-done(((bf16[384,1024]{1,0:T(8,128)(2,1)}), bf16[768,1024]{1,0:T(8,128)(2,1)}) %all-gather.4.cloned.1.call-update) | async-done | bytes 1572880 | tf_op jit(solution)/shard_map/all_gather | solution.py:104
  340.4 8.0 %fusion.3 = f32[768,1792]{1,0:T(8,128)} fusion(bf16[768,1024]{1,0:T(8,128)(2,1)} %all-gather.4.cloned.1.call-done, bf16[1,1792,1024]{2,1,0:T(8,128)(2,1)} %param.12), kind=kOutput, calls=%fused_computation.16 | convolution fusion | flops 2818572288 | bytes 10747904 | tf_op jit(solution)/shard_map/rf,df->rd/dot_general | solution.py:121
  348.4 7.2 %add_convert_fusion = bf16[768,1792]{1,0:T(8,128)(2,1)} fusion(f32[768,1792]{1,0:T(8,128)} %fusion.3, bf16[768,1024]{1,0:T(8,128)(2,1)S(1)} %bitcast.74, bf16[1,1792,1024]{2,1,0:T(8,128)(2,1)} %param.11), kind=kOutput, calls=%fused_computation.9 | convolution fusion | flops 2821324800 | bytes 13500416 | tf_op jit(solution)/shard_map/rf,df->rd/dot_general | solution.py:118
  355.6 5.2 %all-to-all-start.7 = ((bf16[2,384,1792]{2,1,0:T(8,128)(2,1)}), bf16[2,384,1792]{2,1,0:T(8,128)(2,1)}, u32[]{:S(2)}, u32[]{:S(2)}) async-start(bf16[2,384,1792]{2,1,0:T(8,128)(2,1)} %bitcast.73), calls=%async_computation.8 | async-start | bytes 5505024 | tf_op jit(solution)/shard_map/all_to_all | solution.py:129
  362.1 20.8 %all-gather.6.cloned.1.call-done = bf16[768,1024]{1,0:T(8,128)(2,1)} async-done(((bf16[384,1024]{1,0:T(8,128)(2,1)}), bf16[768,1024]{1,0:T(8,128)(2,1)}) %all-gather.6.cloned.1.call-update) | async-done | bytes 1572880 | tf_op jit(solution)/shard_map/all_gather | solution.py:102
  382.9 6.5 %multiply_reduce_fusion = f32[768]{0:T(1024)S(1)} fusion(bf16[768,1792]{1,0:T(8,128)(2,1)} %bitcast.9, bf16[768,1024]{1,0:T(8,128)(2,1)} %all-gather.6.cloned.1.call-done, bf16[1,1792,1024]{2,1,0:T(8,128)(2,1)} %param.13), kind=kOutput, calls=%fused_computation.8 | convolution fusion | flops 2822700288 | bytes 7998464 | tf_op jit(solution)/shard_map/rf,df->rd/dot_general | solution.py:124
  389.4 13.4 %all-reduce.1 = bf16[768]{0:T(1024)(128)(2,1)S(1)} all-reduce(f32[768]{0:T(1024)S(1)} %multiply_reduce_fusion), channel_id=3, replica_groups=mesh['expert'=64,'dp'=2] {'dp'}, use_global_device_ids=true, to_apply=%region_6.7.clone | all-reduce | flops 768 | bytes 4608
  403.7 10.6 %all-to-all-start.9 = ((bf16[64,1,6]{2,1,0:T(2,128)(2,1)}), bf16[64,1,6]{2,1,0:T(2,128)(2,1)S(1)}, u32[]{:S(2)}, u32[]{:S(2)}) async-start(bf16[64,1,6]{2,1,0:T(2,128)(2,1)} %all_to_all.96), calls=%async_computation.10 | async-start | bytes 65536 | tf_op jit(solution)/shard_map/all_to_all | solution.py:138
  414.3 6.1 %copy.22 = bf16[384,2,1792]{2,1,0:T(2,128)(2,1)} copy(bf16[384,2,1792]{2,0,1:T(8,128)(2,1)} %bitcast.14) | data formatting | bytes 5505024 | tf_op jit(solution)/shard_map/all_to_all | solution.py:129
  420.5 7.6 %reshape.80 = bf16[64,6,3584]{2,1,0:T(8,128)(2,1)} reshape(bf16[384,2,1792]{2,1,0:T(2,128)(2,1)} %copy.22) | data formatting | bytes 5505024 | tf_op jit(solution)/shard_map/reshape | solution.py:132
  428.1 10.5 %all-to-all-start.8 = ((bf16[64,6,3584]{2,1,0:T(8,128)(2,1)}), bf16[64,6,3584]{2,1,0:T(8,128)(2,1)}, u32[]{:S(2)}, u32[]{:S(2)}) async-start(bf16[64,6,3584]{2,1,0:T(8,128)(2,1)} %reshape.80), calls=%async_computation.9 | async-start | bytes 7340032 | tf_op jit(solution)/shard_map/all_to_all | solution.py:131
  438.6 43.8 %all-gather = bf16[2,1,384]{2,1,0:T(2,128)(2,1)S(1)} all-gather(bf16[1,1,384]{2,1,0:T(2,128)(2,1)S(1)} %reshape.145), channel_id=1, replica_groups=mesh['expert'=64,'dp'=2] {'dp'}, dimensions={0}, use_global_device_ids=true | all-gather | bytes 2304 | tf_op jit(solution)/shard_map/all_gather | solution.py:105
  482.5 6.4 %fusion.13 = bf16[1,1792,1024]{2,1,0:T(8,128)(2,1)} fusion(bf16[2,384,1024]{2,1,0:T(8,128)(2,1)S(1)} %all-to-all-done.6, bf16[384,2,1792]{0,2,1:T(8,128)(2,1)} %all-to-all-done.3), kind=kOutput, calls=%fused_computation.28 | convolution fusion | flops 2820407296 | bytes 7995392 | tf_op jit(solution)/shard_map/rd,rf->df/dot_general | solution.py:111
  493.4 6.4 %fusion.12 = bf16[1,1792,1024]{2,1,0:T(8,128)(2,1)} fusion(bf16[768,1792]{1,0:T(8,128)(2,1)} %bitcast.9, bf16[768,1024]{1,0:T(8,128)(2,1)S(1)} %copy-done.9, f32[768]{0:T(1024)S(1)} %reshape.147), kind=kOutput, calls=%fused_computation.27 | convolution fusion | flops 2822766592 | bytes 7998464 | tf_op jit(solution)/shard_map/rd,rf->df/dot_general | solution.py:117
  501.8 5.6 %reshape.81 = bf16[384,3584]{1,0:T(8,128)(2,1)} reshape(bf16[64,6,3584]{2,1,0:T(8,128)(2,1)} %all-to-all-done.8) | data formatting | bytes 5505024 | tf_op jit(solution)/shard_map/reshape | solution.py:146
  507.4 5.1 gather_fusion.3
  (80 shorter events, 62.9 us)
Async XLA Ops:
  7.2 3.5 copy-start
  14.6 5.5 %copy-start.3 = (bf16[128,3584]{1,0:T(8,128)(2,1)S(1)}, bf16[128,3584]{1,0:T(8,128)(2,1)}, u32[]{:S(2)}) copy-start(bf16[128,3584]{1,0:T(8,128)(2,1)} %param.8) | copy-start | bytes 2752516
  89.2 58.7 %all-to-all-start.4 = ((bf16[64,6,3584]{2,1,0:T(8,128)(2,1)}), bf16[64,6,3584]{2,1,0:T(8,128)(2,1)}, u32[]{:S(2)}, u32[]{:S(2)}) async-start(bf16[64,6,3584]{2,1,0:T(8,128)(2,1)} %get-tuple-element.11), calls=%async_computation.4 | async-start | bytes 7340032 | tf_op jit(solution)/shard_map/all_to_all | solution.py:60
  147.9 38.0 %all-to-all-start.3 = ((bf16[384,2,1792]{0,2,1:T(8,128)(2,1)}), bf16[384,2,1792]{0,2,1:T(8,128)(2,1)}, u32[]{:S(2)}, u32[]{:S(2)}) async-start(bf16[384,2,1792]{0,2,1:T(8,128)(2,1)} %copy.19), calls=%async_computation.3 | async-start | bytes 5505024 | tf_op jit(solution)/shard_map/all_to_all | solution.py:79
  185.9 37.4 %all-to-all-start.5 = ((bf16[384,2,1792]{2,0,1:T(8,128)(2,1)}), bf16[384,2,1792]{2,0,1:T(8,128)(2,1)}, u32[]{:S(2)}, u32[]{:S(2)}) async-start(bf16[384,2,1792]{2,0,1:T(8,128)(2,1)} %copy.21), calls=%async_computation.5 | async-start | bytes 5505024 | tf_op jit(solution)/shard_map/all_to_all | solution.py:80
  191.1 103.3 %reduce-scatter.2.cloned.1.call-start = ((), (), s32[]{:S(2)}) async-start(), calls=%async_computation.11 | async-start | bytes 7077888 | tf_op jit(solution)/shard_map/reduce_scatter | solution.py:88
  195.9 6.0 %copy-start.4 = (bf16[2,384,1792]{2,1,0:T(8,128)(2,1)S(1)}, bf16[2,384,1792]{2,1,0:T(8,128)(2,1)}, u32[]{:S(2)}) copy-start(bf16[2,384,1792]{2,1,0:T(8,128)(2,1)} %copy.20) | copy-start | bytes 8257540
  195.9 6.0 %copy-start.7 = (bf16[1,1792,1024]{2,1,0:T(8,128)(2,1)S(1)}, bf16[1,1792,1024]{2,1,0:T(8,128)(2,1)}, u32[]{:S(2)}) copy-start(bf16[1,1792,1024]{2,1,0:T(8,128)(2,1)} %param.12) | copy-start | bytes 11010052
  223.3 6.0 %copy-start.6 = (bf16[768,1024]{1,0:T(8,128)(2,1)S(1)}, bf16[768,1024]{1,0:T(8,128)(2,1)}, u32[]{:S(2)}) copy-start(bf16[768,1024]{1,0:T(8,128)(2,1)} %fusion.19) | copy-start | bytes 4718596
  231.6 0.7 copy-start.2
  250.7 7.0 %all-to-all-start.1 = ((bf16[2,2,192]{2,1,0:T(2,128)(2,1)}), bf16[2,2,192]{2,1,0:T(2,128)(2,1)S(1)}, u32[]{:S(2)}, u32[]{:S(2)}) async-start(bf16[2,2,192]{2,1,0:T(2,128)(2,1)} %reshape.158), calls=%async_computation.1 | async-start | bytes 4096 | tf_op jit(solution)/shard_map/all_to_all | solution.py:81
  253.9 86.5 %all-gather.4.cloned.1.call-start = ((), (), s32[]{:S(2)}) async-start(), calls=%async_computation.12 | async-start | bytes 2359296 | tf_op jit(solution)/shard_map/all_gather | solution.py:104
  300.1 48.2 %all-to-all-start.6 = ((bf16[2,384,1024]{2,1,0:T(8,128)(2,1)}), bf16[2,384,1024]{2,1,0:T(8,128)(2,1)S(1)}, u32[]{:S(2)}, u32[]{:S(2)}) async-start(bf16[2,384,1024]{2,1,0:T(8,128)(2,1)} %pad_maximum_fusion.1), calls=%async_computation.7 | async-start | bytes 3145728 | tf_op jit(solution)/shard_map/all_to_all | solution.py:7
  303.8 79.1 %all-gather.6.cloned.1.call-start = ((), (), s32[]{:S(2)}) async-start(), calls=%async_computation.13 | async-start | bytes 2359296 | tf_op jit(solution)/shard_map/all_gather | solution.py:102
  355.6 5.2 %copy-start.10 = (u32[128]{0:T(128)S(1)}, u32[128]{0:T(128)}, u32[]{:S(2)}) copy-start(u32[128]{0:T(128)} %constant.54) | copy-start | bytes 1540
  355.6 48.1 %all-to-all-start.7 = ((bf16[2,384,1792]{2,1,0:T(8,128)(2,1)}), bf16[2,384,1792]{2,1,0:T(8,128)(2,1)}, u32[]{:S(2)}, u32[]{:S(2)}) async-start(bf16[2,384,1792]{2,1,0:T(8,128)(2,1)} %bitcast.73), calls=%async_computation.8 | async-start | bytes 5505024 | tf_op jit(solution)/shard_map/all_to_all | solution.py:129
  403.7 24.4 %all-to-all-start.9 = ((bf16[64,1,6]{2,1,0:T(2,128)(2,1)}), bf16[64,1,6]{2,1,0:T(2,128)(2,1)S(1)}, u32[]{:S(2)}, u32[]{:S(2)}) async-start(bf16[64,1,6]{2,1,0:T(2,128)(2,1)} %all_to_all.96), calls=%async_computation.10 | async-start | bytes 65536 | tf_op jit(solution)/shard_map/all_to_all | solution.py:138
  428.1 73.8 %all-to-all-start.8 = ((bf16[64,6,3584]{2,1,0:T(8,128)(2,1)}), bf16[64,6,3584]{2,1,0:T(8,128)(2,1)}, u32[]{:S(2)}, u32[]{:S(2)}) async-start(bf16[64,6,3584]{2,1,0:T(8,128)(2,1)} %reshape.80), calls=%async_computation.9 | async-start | bytes 7340032 | tf_op jit(solution)/shard_map/all_to_all | solution.py:131
  482.5 6.4 %copy-start.5 = (bf16[2,384,1792]{2,1,0:T(8,128)(2,1)S(1)}, bf16[2,384,1792]{2,1,0:T(8,128)(2,1)}, u32[]{:S(2)}) copy-start(bf16[2,384,1792]{2,1,0:T(8,128)(2,1)} %copy.20) | copy-start | bytes 8257540
  482.5 6.4 %copy-start.8 = (bf16[768,1024]{1,0:T(8,128)(2,1)S(1)}, bf16[768,1024]{1,0:T(8,128)(2,1)}, u32[]{:S(2)}) copy-start(bf16[768,1024]{1,0:T(8,128)(2,1)} %all-gather.4.cloned.1.call-done) | copy-start | bytes 4718596
  488.9 4.5 copy-start.9
  501.8 10.7 %copy-start.1 = (bf16[128,3584]{1,0:T(8,128)(2,1)S(1)}, bf16[128,3584]{1,0:T(8,128)(2,1)}, u32[]{:S(2)}) copy-start(bf16[128,3584]{1,0:T(8,128)(2,1)} %param.7) | copy-start | bytes 2752516
Sparse Core Ops, SparseCore 0:
  231.7 62.5 reduce-scatter.1
  299.0 41.3 all-gather.3
  342.7 40.1 all-gather.5
